TPU v7x, 32 devices: a whole 2x2x4 slice. The times are simulated.
32 devices in a mesh: row: 4 (over x, core), col: 8 (over z, y).
Axes of the slice: x: 2, y: 2, z: 4, core: 2. Of those that a mesh axis runs over, the one named last changes fastest.
Arguments:
- slices: float32 [8, 8192, 8192], P(None, 'row', 'col'), may hold values from -6 to 6
- basis: float32 [8192, 128], P('col'), may hold values from -0.0625 to 0.0625
Outputs:
- gram: float32 [8192, 8192], P('row', 'col')
All inputs are finite; a program needn't handle non-finite values.
Results may differ from a plain program's by a relative error of at most 0.0001.
Values sent between devices are 32-bit elements; how exact they have to be, the bound alone decides.
A program may use at most 192 MiB of HBM per device.

v0:
```python
import jax
import jax.numpy as jnp
from jax import lax
from jax.sharding import PartitionSpec as P


def from_root(block, axis, owner):
    block = jnp.where(lax.axis_index(axis) == owner, block, jnp.zeros_like(block))
    return lax.psum(block, axis)


def shards(slices, basis):
    count = slices.shape[0]
    row_block = slices.shape[1]
    col_block = slices.shape[2]
    rank = basis.shape[1]
    partial_value = jnp.einsum(
        "kac,cr->kar",
        slices,
        basis,
        precision=lax.Precision.HIGHEST,
        preferred_element_type=jnp.float32,
    )
    projected = lax.psum(partial_value, "col")
    column_index = lax.axis_index("col")
    first_col = column_index * col_block
    owner_row = first_col // row_block
    local_start = first_col % row_block
    own_slab = lax.dynamic_slice_in_dim(projected, local_start, col_block, 1)
    column_slab = from_root(own_slab, "row", owner_row)
    scale = 1.0 / jnp.sqrt(jnp.float32(count * rank))
    outer = jnp.einsum(
        "kar,kbr->ab",
        projected,
        column_slab,
        precision=lax.Precision.HIGHEST,
        preferred_element_type=jnp.float32,
    )
    return outer * scale


def solution(mesh):
    placed = (P(None, "row", "col"), P("col", None))
    return jax.shard_map(
        shards, mesh=mesh, in_specs=placed, out_specs=P("row", "col"), check_vma=False
    )
```

profile of v0, /device:TPU:7, one launch (start us, length us, event | category | flops | bytes accessed | tf_op | source)
XLA Modules:
  0.0 465.6 jit_solution(3804304047926928613)
XLA Ops:
  6.5 0.0 copy-start
  6.5 0.0 all-reduce.3.cloned.1.call-start
  6.5 1.0 copy-done
  7.6 59.0 %fusion = f32[8,2048,128]{2,1,0:T(8,128)} fusion(f32[8,2048,1024]{2,1,0:T(8,128)} %param.2, f32[1024,128]{1,0:T(8,128)S(1)} %copy-done), kind=kOutput, calls=%fused_computation.2 | convolution fusion | flops 25769803776 | bytes 76021760 | tf_op jit(solution)/shard_map/kac,cr->kar/dot_general | solution.py:17
  66.6 0.0 all-reduce.3.cloned.1.call-update
  66.6 0.2 all-reduce.5.cloned.1.call-start
  66.9 271.4 %all-reduce.3.cloned.1.call-done = f32[8,2048,128]{2,1,0:T(8,128)} async-done(((f32[8,2048,128]{2,1,0:T(8,128)}), f32[8,2048,128]{2,1,0:T(8,128)}) %all-reduce.3.cloned.1.call-update) | async-done | bytes 8388624 | tf_op jit(solution)/shard_map/psum | solution.py:24
  338.3 4.5 dynamic-slice_select_fusion
  342.8 0.0 all-reduce.5.cloned.1.call-update
  342.9 84.1 %all-reduce.5.cloned.1.call-done = f32[8,1024,128]{2,1,0:T(8,128)} async-done(((f32[8,1024,128]{2,1,0:T(8,128)}), f32[8,1024,128]{2,1,0:T(8,128)}) %all-reduce.5.cloned.1.call-update) | async-done | bytes 4194320 | tf_op jit(solution)/shard_map/psum | solution.py:9
  427.0 31.8 %bitcast_multiply_fusion = f32[2048,1024]{1,0:T(8,128)} fusion(f32[8,2048,128]{2,1,0:T(8,128)} %all-reduce.3.cloned.1.call-done, f32[8,1024,128]{2,1,0:T(8,128)} %all-reduce.5.cloned.1.call-done), kind=kOutput, calls=%fused_computation | convolution fusion | flops 25771900928 | bytes 20971520 | tf_op jit(solution)/shard_map/kar,kbr->ab/dot_general | solution.py:32
Async XLA Ops:
  6.5 1.0 copy-start
  6.5 331.8 %all-reduce.3.cloned.1.call-start = ((), (), s32[]{:S(2)}) async-start(), calls=%async_computation | async-start | bytes 16777216 | tf_op jit(solution)/shard_map/psum | solution.py:24
  66.6 360.3 %all-reduce.5.cloned.1.call-start = ((), (), s32[]{:S(2)}) async-start(), calls=%async_computation.1 | async-start | bytes 8388608 | tf_op jit(solution)/shard_map/psum | solution.py:9
Sparse Core Ops, SparseCore 0:
  66.7 271.5 all-reduce.2
  343.0 83.9 all-reduce.4
where the time goes:
time: 468 us; the launch traced here: 466 us
  waiting for transfers between devices  356 us (76%)
  matrix products  90.8 us (19%)
  between operations  13.4 us (3%)
    psum x1, waiting for transfers between devices, shards(): projected = lax.psum(partial_value, 'col')  271 us
    psum x1, waiting for transfers between devices, from_root(): return lax.psum(block, axis)  84.1 us
    dot_general x1, matrix products, shards(): jnp.einsum('kac,cr->kar', slices, basis, precision=lax.Precision.HIGHEST,...  59 us
    dot_general x1, matrix products, shards(): jnp.einsum('kar,kbr->ab', projected, column_slab, precision=lax.Precision...  31.8 us
  transfers between devices with their start and end apart: 2, of which 2 were waited for; matrix products, arithmetic and copies ran while one was open for 0% of the time, Pallas kernels for 0%

commit v1 on v0

v1 whole, which is shorter than its diff:
```python
import functools

import jax
import jax.numpy as jnp
from jax import lax
from jax.experimental import pallas as pl
from jax.experimental.pallas import tpu as pltpu
from jax.sharding import PartitionSpec as P

MESH = pl.DeviceIdType.MESH
QUARTERS = 4
LINE = 4
LAG_REDUCE, LAG_ROOT, LAG_SPREAD, LAG_DONE = 2, 4, 6, 8


def split(value):
    high = value.astype(jnp.bfloat16)
    low = (value - high.astype(jnp.float32)).astype(jnp.bfloat16)
    return high, low


def gram_kernel(
    scale, slices, basis, out,
    part, fin, y_in, za_in, zb_in, yb_in, slab, stream, factor, slab_t, acc,
    stream_sem, y_s, y_r, za_s, za_r, zb_s, zb_r, yb_s, yb_r,
    ca_s, ca_r, cb_s, cb_r, yg_s, yg_r, sa_s, sa_r, sb_s, sb_r, out_sem,
):
    count, rows, depth = slices.shape
    rank = basis.shape[1]
    pairs = count // 2
    segments = pairs * QUARTERS
    half = rows // 2
    a_rows = half // QUARTERS
    b_rows = rows // QUARTERS
    row = lax.axis_index("row")
    col = lax.axis_index("col")
    z, y = col // 2, col % 2
    mate = {"col": z * 2 + 1 - y}
    others = [{"row": lax.rem(row + i, 4)} for i in (1, 2, 3)]
    owner = row == z
    inner = (z > 0) & (z < LINE - 1)

    def at_z(position):
        return {"col": position * 2 + y}

    def place(s):
        return s // QUARTERS, s % QUARTERS

    def root_of(s):
        return LINE // 2 - 1 + s % 2

    def a_part(s, side):
        p, q = place(s)
        return p, pl.ds(pl.multiple_of(side * half + q * a_rows, a_rows), a_rows)

    def b_part(s):
        p, q = place(s)
        return pairs + p, pl.ds(pl.multiple_of(q * b_rows, b_rows), b_rows)

    def remote(src, dst, send, recv, device):
        return pltpu.make_async_remote_copy(
            src_ref=src, dst_ref=dst, send_sem=send, recv_sem=recv,
            device_id=device, device_id_type=MESH,
        )

    def stream_copies(s):
        slot = s % 2
        k, first = a_part(s, 0)
        _, second = a_part(s, 1)
        kb, all_b = b_part(s)
        return [
            pltpu.make_async_copy(slices.at[k, first], stream.at[slot, pl.ds(0, a_rows)], stream_sem.at[slot, 0]),
            pltpu.make_async_copy(slices.at[k, second], stream.at[slot, pl.ds(a_rows, a_rows)], stream_sem.at[slot, 1]),
            pltpu.make_async_copy(slices.at[kb, all_b], stream.at[slot, pl.ds(2 * a_rows, b_rows)], stream_sem.at[slot, 2]),
        ]

    def y_copy(s):
        k, there = a_part(s, 1 - y)
        return remote(part.at[k, there], y_in.at[s], y_s.at[s], y_r.at[s], mate)

    def z_copies(s):
        root = root_of(s)
        target = at_z(jnp.where(z < root, z + 1, jnp.maximum(z - 1, 0)))
        slot = jnp.where(z - 1 == root, segments + s // 2, s)
        k, mine = a_part(s, y)
        kb, all_b = b_part(s)
        return [
            remote(part.at[k, mine], za_in.at[slot], za_s.at[s], za_r.at[slot], target),
            remote(part.at[kb, all_b], zb_in.at[slot], zb_s.at[s], zb_r.at[slot], target),
        ]

    def yb_copy(s):
        kb, all_b = b_part(s)
        return remote(part.at[kb, all_b], yb_in.at[s // 2], yb_s.at[s // 2], yb_r.at[s // 2], mate)

    def a_spread(s, way, to):
        k, mine = a_part(s, y)
        return remote(fin.at[k, mine], fin.at[k, mine], ca_s.at[s, way], ca_r.at[s], at_z(to))

    def b_spread(s, way, to):
        kb, all_b = b_part(s)
        return remote(fin.at[kb, all_b], fin.at[kb, all_b], cb_s.at[s, way], cb_r.at[s], at_z(to))

    def y_gather(s, side):
        k, mine = a_part(s, side)
        return remote(fin.at[k, mine], fin.at[k, mine], yg_s.at[s], yg_r.at[s], mate)

    def slab_a(s):
        k, mine = a_part(s, y)
        _, q = place(s)
        return fin.at[k, mine], slab.at[k, pl.ds(pl.multiple_of(q * a_rows, a_rows), a_rows)]

    def slab_b(s):
        kb, all_b = b_part(s)
        _, q = place(s)
        return fin.at[kb, all_b], slab.at[kb, pl.ds(pl.multiple_of((q % 2) * b_rows, b_rows), b_rows)]

    def in_slab(s):
        return (s % QUARTERS) // 2 == y

    for copy in stream_copies(0):
        copy.start()

    high, low = split(basis[...])
    factor[:, :rank] = high
    factor[:, rank:] = low

    barrier = pltpu.get_barrier_semaphore()
    pl.semaphore_signal(barrier, inc=1, device_id=mate, device_id_type=MESH)
    for device in others:
        pl.semaphore_signal(barrier, inc=1, device_id=device, device_id_type=MESH)

    @pl.when(z > 0)
    def _():
        pl.semaphore_signal(barrier, inc=1, device_id=at_z(jnp.maximum(z - 1, 0)), device_id_type=MESH)

    @pl.when(z < LINE - 1)
    def _():
        pl.semaphore_signal(barrier, inc=1, device_id=at_z(jnp.minimum(z + 1, LINE - 1)), device_id_type=MESH)

    pl.semaphore_wait(barrier, jnp.where(inner, 6, 5))
    acc[...] = jnp.zeros_like(acc)

    def project(s):
        slot = s % 2

        @pl.when(s + 1 < segments)
        def _():
            for copy in stream_copies(s + 1):
                copy.start()

        for copy in stream_copies(s):
            copy.wait()
        p, q = place(s)
        for i in range(4):
            high, low = split(stream[slot, i * a_rows:(i + 1) * a_rows, :])
            both = jnp.dot(high, factor[...], preferred_element_type=jnp.float32)
            both += jnp.dot(low, factor[...], preferred_element_type=jnp.float32)
            value = both[:, :rank] + both[:, rank:]
            if i < 2:
                k, there = a_part(s, i)
            else:
                k = pairs + p
                there = pl.ds(pl.multiple_of(q * b_rows + (i - 2) * a_rows, a_rows), a_rows)
            part[k, there, :] = value
        y_copy(s).start()

    def reduce(s):
        root = root_of(s)
        k, mine = a_part(s, y)
        kb, all_b = b_part(s)
        y_copy(s).wait_recv()
        part[k, mine, :] += y_in[s]

        @pl.when(inner)
        def _():
            pltpu.make_async_copy(za_in.at[s], za_in.at[s], za_r.at[s]).wait()
            part[k, mine, :] += za_in[s]
            pltpu.make_async_copy(zb_in.at[s], zb_in.at[s], zb_r.at[s]).wait()
            part[kb, all_b, :] += zb_in[s]

        @pl.when(z != root)
        def _():
            for copy in z_copies(s):
                copy.start()

        @pl.when(z == root)
        def _():
            second = segments + s // 2
            pltpu.make_async_copy(za_in.at[second], za_in.at[second], za_r.at[second]).wait()
            fin[k, mine, :] = part[k, mine, :] + za_in[second]
            a_spread(s, 0, z - 1).start()
            a_spread(s, 1, z + 1).start()
            y_gather(s, y).start()
            pltpu.make_async_copy(zb_in.at[second], zb_in.at[second], zb_r.at[second]).wait()
            part[kb, all_b, :] += zb_in[second]
            yb_copy(s).start()

    def finish_root(s):
        kb, all_b = b_part(s)

        @pl.when(z == root_of(s))
        def _():
            yb_copy(s).wait_recv()
            fin[kb, all_b, :] = part[kb, all_b, :] + yb_in[s // 2]
            b_spread(s, 0, z - 1).start()
            b_spread(s, 1, z + 1).start()

    def spread(s):
        root = root_of(s)
        outer = jnp.clip(jnp.where(z < root, z - 1, z + 1), 0, LINE - 1)

        @pl.when(z != root)
        def _():
            a_spread(s, 0, outer).wait_recv()

            @pl.when(inner)
            def _():
                a_spread(s, 0, outer).start()

            y_gather(s, y).start()

        @pl.when(z != root)
        def _():
            b_spread(s, 0, outer).wait_recv()

            @pl.when(inner)
            def _():
                b_spread(s, 0, outer).start()

        @pl.when(owner)
        def _():
            src, dst = slab_a(s)
            for i, device in enumerate(others):
                remote(src, dst, sa_s.at[s, i], sa_r.at[s], device).start()
            pltpu.make_async_copy(src, dst, sa_r.at[s]).start()

        @pl.when(owner & in_slab(s))
        def _():
            src, dst = slab_b(s)
            for i, device in enumerate(others):
                remote(src, dst, sb_s.at[s, i], sb_r.at[s], device).start()
            pltpu.make_async_copy(src, dst, sb_r.at[s]).start()

    def done(s):
        y_gather(s, 1 - y).wait_recv()
        src, dst = slab_a(s)
        pltpu.make_async_copy(src, dst, sa_r.at[s]).wait()

        @pl.when(in_slab(s))
        def _():
            src, dst = slab_b(s)
            pltpu.make_async_copy(src, dst, sb_r.at[s]).wait()

    def out_copy(j):
        here = pl.ds(pl.multiple_of(j * b_rows, b_rows), b_rows)
        return pltpu.make_async_copy(acc.at[here], out.at[here], out_sem.at[j])

    def multiply(s):
        p, j = place(s)

        @pl.when(j == 0)
        def _():
            for i, k in enumerate((p, pairs + p)):
                high, low = split((slab[k] * scale).T)
                slab_t[i * rank:(i + 1) * rank, :] = high
                slab_t[(2 + i) * rank:(3 + i) * rank, :] = high
                slab_t[(4 + i) * rank:(5 + i) * rank, :] = low

        for i in range(2):
            here = pl.ds(pl.multiple_of(j * b_rows + i * a_rows, a_rows), a_rows)
            high, low = split(jnp.concatenate([fin[p, here, :], fin[pairs + p, here, :]], axis=1))
            left = jnp.concatenate([high, low, high], axis=1)
            acc[here, :] += jnp.dot(left, slab_t[...], preferred_element_type=jnp.float32)

        @pl.when(p == pairs - 1)
        def _():
            out_copy(j).start()

    def stage(action, s):
        pl.when((s >= 0) & (s < segments))(lambda: action(s))

    def body(t, carry):
        stage(spread, t - LAG_SPREAD)
        stage(finish_root, t - LAG_ROOT)
        stage(reduce, t - LAG_REDUCE)
        stage(project, t)
        stage(done, t - LAG_DONE)
        stage(multiply, t - LAG_DONE - QUARTERS + 1)
        return carry

    lax.fori_loop(0, segments + LAG_DONE + QUARTERS - 1, body, 0)

    def drain(s, carry):
        root = root_of(s)
        y_copy(s).wait_send()
        y_gather(s, y).wait_send()

        @pl.when(z != root)
        def _():
            for copy in z_copies(s):
                copy.wait_send()

            @pl.when(inner)
            def _():
                outer = jnp.where(z < root, z - 1, z + 1)
                a_spread(s, 0, outer).wait_send()
                b_spread(s, 0, outer).wait_send()

        @pl.when(z == root)
        def _():
            yb_copy(s).wait_send()
            for way, to in ((0, z - 1), (1, z + 1)):
                a_spread(s, way, to).wait_send()
                b_spread(s, way, to).wait_send()

        @pl.when(owner)
        def _():
            src, dst = slab_a(s)
            for i, device in enumerate(others):
                remote(src, dst, sa_s.at[s, i], sa_r.at[s], device).wait_send()

        @pl.when(owner & in_slab(s))
        def _():
            src, dst = slab_b(s)
            for i, device in enumerate(others):
                remote(src, dst, sb_s.at[s, i], sb_r.at[s], device).wait_send()

        return carry

    lax.fori_loop(0, segments, drain, 0)
    for j in range(QUARTERS):
        out_copy(j).wait()


def gram_call(slices, basis):
    count, rows, depth = slices.shape
    rank = basis.shape[1]
    columns = rows // 2
    segments = count // 2 * QUARTERS
    roots = segments // 2
    a_rows = rows // (2 * QUARTERS)
    b_rows = rows // QUARTERS
    f32, bf16 = jnp.float32, jnp.bfloat16
    dma = pltpu.SemaphoreType.DMA
    scale = 1.0 / float(count * rank) ** 0.5
    return pl.pallas_call(
        functools.partial(gram_kernel, scale),
        out_shape=jax.ShapeDtypeStruct((rows, columns), f32),
        in_specs=[pl.BlockSpec(memory_space=pl.ANY), pl.BlockSpec(memory_space=pltpu.VMEM)],
        out_specs=pl.BlockSpec(memory_space=pl.ANY),
        scratch_shapes=[
            pltpu.VMEM((count, rows, rank), f32),
            pltpu.VMEM((count, rows, rank), f32),
            pltpu.VMEM((segments, a_rows, rank), f32),
            pltpu.VMEM((segments + roots, a_rows, rank), f32),
            pltpu.VMEM((segments + roots, b_rows, rank), f32),
            pltpu.VMEM((roots, b_rows, rank), f32),
            pltpu.VMEM((count, columns, rank), f32),
            pltpu.VMEM((2, 2 * a_rows + b_rows, depth), f32),
            pltpu.VMEM((depth, 2 * rank), bf16),
            pltpu.VMEM((6 * rank, columns), bf16),
            pltpu.VMEM((rows, columns), f32),
            dma((2, 3)),
            dma((segments,)), dma((segments,)),
            dma((segments,)), dma((segments + roots,)),
            dma((segments,)), dma((segments + roots,)),
            dma((roots,)), dma((roots,)),
            dma((segments, 2)), dma((segments,)),
            dma((segments, 2)), dma((segments,)),
            dma((segments,)), dma((segments,)),
            dma((segments, 3)), dma((segments,)),
            dma((segments, 3)), dma((segments,)),
            dma((QUARTERS,)),
        ],
        compiler_params=pltpu.CompilerParams(
            collective_id=0, has_side_effects=True, vmem_limit_bytes=62 * 2**20
        ),
        cost_estimate=pl.CostEstimate(
            flops=2 * count * rows * rank * (4 * depth + 3 * columns),
            bytes_accessed=4 * (count * rows * depth + rows * columns),
            transcendentals=0,
        ),
    )(slices, basis)


def from_root(block, axis, owner):
    block = jnp.where(lax.axis_index(axis) == owner, block, jnp.zeros_like(block))
    return lax.psum(block, axis)


def general(slices, basis):
    count = slices.shape[0]
    row_block = slices.shape[1]
    col_block = slices.shape[2]
    rank = basis.shape[1]
    partial_value = jnp.einsum(
        "kac,cr->kar",
        slices,
        basis,
        precision=lax.Precision.HIGHEST,
        preferred_element_type=jnp.float32,
    )
    projected = lax.psum(partial_value, "col")
    first_col = lax.axis_index("col") * col_block
    owner_row = first_col // row_block
    own_slab = lax.dynamic_slice_in_dim(projected, first_col % row_block, col_block, 1)
    column_slab = from_root(own_slab, "row", owner_row)
    scale = 1.0 / jnp.sqrt(jnp.float32(count * rank))
    outer = jnp.einsum(
        "kar,kbr->ab",
        projected,
        column_slab,
        precision=lax.Precision.HIGHEST,
        preferred_element_type=jnp.float32,
    )
    return outer * scale


def solution(mesh):
    placed = (P(None, "row", "col"), P("col", None))
    lined = mesh.shape["row"] == LINE and mesh.shape["col"] == 2 * LINE
    return jax.shard_map(
        gram_call if lined else general,
        mesh=mesh, in_specs=placed, out_specs=P("row", "col"), check_vma=False,
    )
```

time: 468 us -> 383 us (0.82)
  Pallas kernels: 0 us -> 374 us
  waiting for transfers between devices: 356 us -> 0 us
  matrix products: 90.8 us -> 0 us
  between operations: 13.4 us -> 0.01 us
  local copies, waits for them, and re-layouts: 1.04 us -> 8.44 us
    pallas_call x0 -> x1, Pallas kernels: none -> 374 us  [gram_call(): pl.pallas_call(functools.partial(gram_kernel, scale), out_shape=jax.Shape...]
    psum x2 -> x0, waiting for transfers between devices: 356 us -> none  [the longest x1 271 us: shards(): projected = lax.psum(partial_value, 'col')]
    dot_general x2 -> x0, matrix products: 90.8 us -> none  [the longest x1 59 us: shards(): jnp.einsum('kac,cr->kar', slices, basis, precision=lax.Precision.HIGHEST,...]
    unnamed x2 -> x1, local copies, waits for them, and re-layouts: 1.04 us -> 8.44 us
  transfers between devices with their start and end apart: 2 -> 0, of which waited for: 2 -> 0; matrix products, arithmetic and copies ran while one was open for 0% -> 0% of each run, Pallas kernels for 0% -> 0%
where the time goes in v1:
time: 383 us
  Pallas kernels  374 us (98%)
  local copies, waits for them, and re-layouts  8.44 us (2%)
    pallas_call x1, Pallas kernels, gram_call(): pl.pallas_call(functools.partial(gram_kernel, scale), out_shape=jax.Shape...  374 us
    unnamed x1, local copies, waits for them, and re-layouts  8.44 us

profile of v1, /device:TPU:7, one launch (start us, length us, event | category | flops | bytes accessed | tf_op | source)
XLA Modules:
  0.0 382.8 jit_solution(9712396820937040636)
XLA Ops:
  0.0 374.4 %shard_map.28 = f32[2048,1024]{1,0:T(8,128)} custom-call(f32[8,2048,1024]{2,1,0:T(8,128)} %slices.1, f32[1024,128]{1,0:T(8,128)} %basis.1), custom_call_target="tpu_custom_call" | custom-call | flops 30064771072 | bytes 75497472 | tf_op jit(solution)/shard_map/pallas_call | solution.py:347
  374.4 8.4 %copy.4 = f32[2048,1024]{1,0:T(8,128)} copy(f32[2048,1024]{1,0:T(8,128)} %shard_map.28) | data formatting | bytes 16777216

commit v2 on v1

--- a/solution.py
+++ b/solution.py
@@ -8,9 +8,9 @@
 from jax.sharding import PartitionSpec as P
 
 MESH = pl.DeviceIdType.MESH
-QUARTERS = 4
+PIECES = 8
 LINE = 4
-LAG_REDUCE, LAG_ROOT, LAG_SPREAD, LAG_DONE = 2, 4, 6, 8
+LAG_END, LAG_INNER, LAG_ROOT, LAG_FINISH, LAG_SPREAD, LAG_OUTER, LAG_DONE = 2, 4, 6, 8, 10, 12, 14
 
 
 def split(value):
@@ -28,10 +28,10 @@
     count, rows, depth = slices.shape
     rank = basis.shape[1]
     pairs = count // 2
-    segments = pairs * QUARTERS
+    segments = pairs * PIECES
     half = rows // 2
-    a_rows = half // QUARTERS
-    b_rows = rows // QUARTERS
+    a_rows = half // PIECES
+    b_rows = rows // PIECES
     row = lax.axis_index("row")
     col = lax.axis_index("col")
     z, y = col // 2, col % 2
@@ -44,7 +44,7 @@
         return {"col": position * 2 + y}
 
     def place(s):
-        return s // QUARTERS, s % QUARTERS
+        return s // PIECES, s % PIECES
 
     def root_of(s):
         return LINE // 2 - 1 + s % 2
@@ -113,10 +113,10 @@
     def slab_b(s):
         kb, all_b = b_part(s)
         _, q = place(s)
-        return fin.at[kb, all_b], slab.at[kb, pl.ds(pl.multiple_of((q % 2) * b_rows, b_rows), b_rows)]
+        return fin.at[kb, all_b], slab.at[kb, pl.ds(pl.multiple_of(q % (PIECES // 2) * b_rows, b_rows), b_rows)]
 
     def in_slab(s):
-        return (s % QUARTERS) // 2 == y
+        return (s % PIECES) // (PIECES // 2) == y
 
     for copy in stream_copies(0):
         copy.start()
@@ -165,36 +165,51 @@
             part[k, there, :] = value
         y_copy(s).start()
 
-    def reduce(s):
-        root = root_of(s)
-        k, mine = a_part(s, y)
-        kb, all_b = b_part(s)
-        y_copy(s).wait_recv()
-        part[k, mine, :] += y_in[s]
-
-        @pl.when(inner)
-        def _():
-            pltpu.make_async_copy(za_in.at[s], za_in.at[s], za_r.at[s]).wait()
-            part[k, mine, :] += za_in[s]
-            pltpu.make_async_copy(zb_in.at[s], zb_in.at[s], zb_r.at[s]).wait()
-            part[kb, all_b, :] += zb_in[s]
-
-        @pl.when(z != root)
-        def _():
+    def arrive(buffer, slot, sem):
+        pltpu.make_async_copy(buffer.at[slot], buffer.at[slot], sem.at[slot]).wait()
+
+    def reduce_end(s):
+        k, mine = a_part(s, y)
+
+        @pl.when(jnp.logical_not(inner))
+        def _():
+            y_copy(s).wait_recv()
+            part[k, mine, :] += y_in[s]
             for copy in z_copies(s):
                 copy.start()
 
-        @pl.when(z == root)
-        def _():
-            second = segments + s // 2
-            pltpu.make_async_copy(za_in.at[second], za_in.at[second], za_r.at[second]).wait()
-            fin[k, mine, :] = part[k, mine, :] + za_in[second]
+    def reduce_inner(s):
+        k, mine = a_part(s, y)
+        kb, all_b = b_part(s)
+
+        @pl.when(inner & (z != root_of(s)))
+        def _():
+            y_copy(s).wait_recv()
+            arrive(za_in, s, za_r)
+            part[k, mine, :] += y_in[s] + za_in[s]
+            arrive(zb_in, s, zb_r)
+            part[kb, all_b, :] += zb_in[s]
+            for copy in z_copies(s):
+                copy.start()
+
+    def reduce_root(s):
+        k, mine = a_part(s, y)
+        kb, all_b = b_part(s)
+        second = segments + s // 2
+
+        @pl.when(z == root_of(s))
+        def _():
+            y_copy(s).wait_recv()
+            arrive(zb_in, s, zb_r)
+            arrive(zb_in, second, zb_r)
+            part[kb, all_b, :] += zb_in[s] + zb_in[second]
+            yb_copy(s).start()
+            arrive(za_in, s, za_r)
+            arrive(za_in, second, za_r)
+            fin[k, mine, :] = (part[k, mine, :] + y_in[s]) + (za_in[s] + za_in[second])
             a_spread(s, 0, z - 1).start()
             a_spread(s, 1, z + 1).start()
             y_gather(s, y).start()
-            pltpu.make_async_copy(zb_in.at[second], zb_in.at[second], zb_r.at[second]).wait()
-            part[kb, all_b, :] += zb_in[second]
-            yb_copy(s).start()
 
     def finish_root(s):
         kb, all_b = b_part(s)
@@ -206,11 +221,11 @@
             b_spread(s, 0, z - 1).start()
             b_spread(s, 1, z + 1).start()
 
-    def spread(s):
+    def spread(s, here):
         root = root_of(s)
         outer = jnp.clip(jnp.where(z < root, z - 1, z + 1), 0, LINE - 1)
 
-        @pl.when(z != root)
+        @pl.when(here & (z != root))
         def _():
             a_spread(s, 0, outer).wait_recv()
 
@@ -220,7 +235,7 @@
 
             y_gather(s, y).start()
 
-        @pl.when(z != root)
+        @pl.when(here & (z != root))
         def _():
             b_spread(s, 0, outer).wait_recv()
 
@@ -228,14 +243,14 @@
             def _():
                 b_spread(s, 0, outer).start()
 
-        @pl.when(owner)
+        @pl.when(here & owner)
         def _():
             src, dst = slab_a(s)
             for i, device in enumerate(others):
                 remote(src, dst, sa_s.at[s, i], sa_r.at[s], device).start()
             pltpu.make_async_copy(src, dst, sa_r.at[s]).start()
 
-        @pl.when(owner & in_slab(s))
+        @pl.when(here & owner & in_slab(s))
         def _():
             src, dst = slab_b(s)
             for i, device in enumerate(others):
@@ -281,15 +296,18 @@
         pl.when((s >= 0) & (s < segments))(lambda: action(s))
 
     def body(t, carry):
-        stage(spread, t - LAG_SPREAD)
-        stage(finish_root, t - LAG_ROOT)
-        stage(reduce, t - LAG_REDUCE)
         stage(project, t)
+        stage(reduce_end, t - LAG_END)
+        stage(reduce_inner, t - LAG_INNER)
+        stage(reduce_root, t - LAG_ROOT)
+        stage(finish_root, t - LAG_FINISH)
+        stage(lambda s: spread(s, inner), t - LAG_SPREAD)
+        stage(lambda s: spread(s, jnp.logical_not(inner)), t - LAG_OUTER)
         stage(done, t - LAG_DONE)
-        stage(multiply, t - LAG_DONE - QUARTERS + 1)
+        stage(multiply, t - LAG_DONE - PIECES + 1)
         return carry
 
-    lax.fori_loop(0, segments + LAG_DONE + QUARTERS - 1, body, 0)
+    lax.fori_loop(0, segments + LAG_DONE + PIECES - 1, body, 0)
 
     def drain(s, carry):
         root = root_of(s)
@@ -329,7 +347,7 @@
         return carry
 
     lax.fori_loop(0, segments, drain, 0)
-    for j in range(QUARTERS):
+    for j in range(PIECES):
         out_copy(j).wait()
 
 
@@ -337,10 +355,10 @@
     count, rows, depth = slices.shape
     rank = basis.shape[1]
     columns = rows // 2
-    segments = count // 2 * QUARTERS
+    segments = count // 2 * PIECES
     roots = segments // 2
-    a_rows = rows // (2 * QUARTERS)
-    b_rows = rows // QUARTERS
+    a_rows = rows // (2 * PIECES)
+    b_rows = rows // PIECES
     f32, bf16 = jnp.float32, jnp.bfloat16
     dma = pltpu.SemaphoreType.DMA
     scale = 1.0 / float(count * rank) ** 0.5
@@ -371,7 +389,7 @@
             dma((segments,)), dma((segments,)),
             dma((segments, 3)), dma((segments,)),
             dma((segments, 3)), dma((segments,)),
-            dma((QUARTERS,)),
+            dma((PIECES,)),
         ],
         compiler_params=pltpu.CompilerParams(
             collective_id=0, has_side_effects=True, vmem_limit_bytes=62 * 2**20

time: 383 us -> 204 us (0.53)
  Pallas kernels: 374 us -> 195 us
    pallas_call x1, Pallas kernels: 374 us -> 195 us  [gram_call(): pl.pallas_call(functools.partial(gram_kernel, scale), out_shape=jax.Shape...]
where the time goes in v2:
time: 204 us; the launch traced here: 203 us
  Pallas kernels  195 us (96%)
  local copies, waits for them, and re-layouts  8.44 us (4%)
    pallas_call x1, Pallas kernels, gram_call(): pl.pallas_call(functools.partial(gram_kernel, scale), out_shape=jax.Shape...  195 us
    unnamed x1, local copies, waits for them, and re-layouts  8.44 us

profile of v2, /device:TPU:7, one launch (start us, length us, event | category | flops | bytes accessed | tf_op | source)
XLA Modules:
  0.0 203.5 jit_solution(12618256808001008247)
XLA Ops:
  0.0 195.0 %shard_map.28 = f32[2048,1024]{1,0:T(8,128)} custom-call(f32[8,2048,1024]{2,1,0:T(8,128)} %slices.1, f32[1024,128]{1,0:T(8,128)} %basis.1), custom_call_target="tpu_custom_call" | custom-call | flops 30064771072 | bytes 75497472 | tf_op jit(solution)/shard_map/pallas_call | solution.py:365
  195.0 8.4 %copy.4 = f32[2048,1024]{1,0:T(8,128)} copy(f32[2048,1024]{1,0:T(8,128)} %shard_map.28) | data formatting | bytes 16777216
